TPU v7x, 256 devices: a whole 4x4x8 slice. The times are simulated.
256 devices in a mesh: tm: 32 (over x_lo, z, core), clip: 8 (over y, x_hi).
Axes of the slice: x: 4 (x_hi: 2, x_lo: 2; x = x_hi * 2 + x_lo), y: 4, z: 8, core: 2. Of those that a mesh axis runs over, the one named last changes fastest.
Arguments:
- frames_in: bfloat16 [768, 256, 1024], P(('clip', 'tm')), parts along dimension 0, may hold values from -6 to 6
- gain_time: float32 [1024], replicated, may hold values from 0.1 to 1.9
- gain_space: float32 [1024], replicated, may hold values from 0.1 to 1.9
- w_tqkv: bfloat16 [1024, 3072], P('tm'), may hold values from -1 to 1, as said below
- w_tout: bfloat16 [1024, 1024], P('tm'), may hold values from -0.1875 to 0.1875
- w_sqkv: bfloat16 [1024, 3072], replicated, may hold values from -1 to 1, as said below
- w_sout: bfloat16 [1024, 1024], replicated, may hold values from -0.1875 to 0.1875
Outputs:
- frames_out: bfloat16 [768, 256, 1024], P(('clip', 'tm')), parts along dimension 0
There are 8 independent parts, one for each index of `clip`. A program takes and returns all parts, laid end to end along the dimension named above; an argument that names none is the same for every part. Nothing has to cross between parts.
Inputs may be any that keep to these rules, and one draw needn't show every extreme that they name: `w_tqkv`: projection weights. `w_sqkv`: projection weights.
All inputs are finite; a program needn't handle non-finite values.
Results may differ from a plain program's by a relative error of at most 0.0051.
Values may be sent and summed in bfloat16 or wider, within the bound.
A program may use at most 128 MiB of HBM per device.

v0:
```python
import jax
import jax.numpy as jnp
from jax import lax
from jax.sharding import PartitionSpec as P

HEADS = 16
HEAD = 64


def norm_tokens(token_rows, gain):
    values = token_rows.astype(jnp.float32)
    average = jnp.mean(values, axis=-1, keepdims=True)
    spread = jnp.mean((values - average) ** 2, axis=-1, keepdims=True)
    return ((values - average) * lax.rsqrt(spread + 1e-05) * gain).astype(jnp.bfloat16)


def time_project(token_rows, w_tqkv):
    zeros_acc = jnp.zeros((token_rows.shape[0], w_tqkv.shape[1]), jnp.float32)

    def add_rows(totals, slab_rows, offset):
        return jnp.dot(token_rows, slab_rows, preferred_element_type=jnp.float32)

    summed = add_rows(zeros_acc, lax.all_gather(w_tqkv, "tm", axis=0, tiled=True), jnp.int32(0))
    return summed.astype(jnp.bfloat16)


def time_output(mixed_rows, w_tout):
    zeros_acc = jnp.zeros((mixed_rows.shape[0], w_tout.shape[1]), jnp.float32)

    def add_rows(totals, slab_rows, offset):
        return jnp.dot(mixed_rows, slab_rows, preferred_element_type=jnp.float32)

    return add_rows(zeros_acc, lax.all_gather(w_tout, "tm", axis=0, tiled=True), jnp.int32(0))


def split_qkv(qkv_rows, frame_count, patch_count):
    shaped = qkv_rows.reshape(frame_count, patch_count, 3, HEADS // 2, 2 * HEAD)
    return (shaped[:, :, 0], shaped[:, :, 1], shaped[:, :, 2])


def attend_time(queries, keys_all, values_all):
    frame_count, patch_count, pairs, packed = queries.shape
    query_five = queries.reshape(frame_count, patch_count, pairs, 2, HEAD)
    key_five = keys_all.reshape(frame_count, patch_count, pairs, 2, HEAD)
    value_five = values_all.reshape(frame_count, patch_count, pairs, 2, HEAD)
    scores = (
        jnp.einsum("fpgjd,epgjd->pgjfe", query_five, key_five, preferred_element_type=jnp.float32)
        * 0.125
    )
    weights = jax.nn.softmax(scores, axis=-1).astype(jnp.bfloat16)
    mixed = jnp.einsum(
        "pgjfe,epgjd->fpgjd", weights, value_five, preferred_element_type=jnp.float32
    )
    return mixed.astype(jnp.bfloat16).reshape(frame_count, patch_count, pairs, packed)


def body(frames_in, gain_time, gain_space, w_tqkv, w_tout, w_sqkv, w_sout):
    frame_count, patch_count, width = frames_in.shape
    token_rows = frames_in.reshape(frame_count * patch_count, width)
    normed_time = norm_tokens(token_rows, gain_time)
    normed_space = norm_tokens(token_rows, gain_space)
    time_qkv = time_project(normed_time, w_tqkv)
    queries, keys_all, values_all = split_qkv(time_qkv, frame_count, patch_count)
    mixed = attend_time(
        lax.all_to_all(queries, "tm", split_axis=1, concat_axis=0, tiled=True),
        lax.all_to_all(keys_all, "tm", split_axis=1, concat_axis=0, tiled=True),
        lax.all_to_all(values_all, "tm", split_axis=1, concat_axis=0, tiled=True),
    )
    time_mixed = lax.all_to_all(mixed, "tm", split_axis=0, concat_axis=1, tiled=True)
    time_branch = time_output(time_mixed.reshape(frame_count * patch_count, width), w_tout)
    space_qkv = jnp.dot(normed_space, w_sqkv, preferred_element_type=jnp.float32).astype(
        jnp.bfloat16
    )
    space_qkv = space_qkv.reshape(frame_count, patch_count, 3, HEADS, HEAD)
    scores = (
        jnp.einsum(
            "fphd,fqhd->fhpq",
            space_qkv[:, :, 0],
            space_qkv[:, :, 1],
            preferred_element_type=jnp.float32,
        )
        * 0.125
    )
    weights = jax.nn.softmax(scores, axis=-1).astype(jnp.bfloat16)
    space_mixed = jnp.einsum(
        "fhpq,fqhd->fphd", weights, space_qkv[:, :, 2], preferred_element_type=jnp.float32
    )
    space_mixed = space_mixed.astype(jnp.bfloat16).reshape(frame_count * patch_count, width)
    space_branch = jnp.dot(space_mixed, w_sout, preferred_element_type=jnp.float32)
    result = token_rows.astype(jnp.float32) + time_branch + space_branch
    return result.astype(jnp.bfloat16).reshape(frame_count, patch_count, width)


def solution(mesh):
    in_specs = (P(("clip", "tm"), None, None), P(), P(), P("tm", None), P("tm", None), P(), P())
    out_specs = P(("clip", "tm"), None, None)
    return jax.shard_map(body, mesh=mesh, in_specs=in_specs, out_specs=out_specs, check_vma=False)
```

profile of v0, /device:TPU:16, one launch (start us, length us, event | category | flops | bytes accessed | tf_op | source)
XLA Modules:
  0.0 356.4 jit_solution(33195694748037621)
XLA Ops:
  6.5 0.7 all-gather.3.cloned.1.call-update
  7.3 1.7 convert_reduce_fusion
  9.0 2.0 fusion.11
  11.0 0.0 copy-done.5
  11.0 0.0 copy-done.6
  11.0 3.8 %fusion.16 = (bf16[768,1024]{1,0:T(8,128)(2,1)}, bf16[768,1024]{1,0:T(8,128)(2,1)}) fusion(bf16[3,256,1024]{2,1,0:T(8,128)(2,1)} %param.7, f32[1024]{0:T(1024)S(1)} %copy-done.5, f32[768]{0:T(1024)S(1)} %rsqrt.13, f32[768]{0:T(1024)S(1)} %div.27, f32[1024]{0:T(1024)S(1)} %copy-done.6), kind=kLoop, calls=%fused_computation.24 | loop fusion | flops 5505024 | bytes 4732928 | tf_op jit(solution)/shard_map/convert_element_type | solution.py:14
  14.7 67.5 %all-gather.3.cloned.1.call-done = bf16[1024,3072]{1,0:T(8,128)(2,1)} async-done(((bf16[32,3072]{1,0:T(8,128)(2,1)}), bf16[1024,3072]{1,0:T(8,128)(2,1)}) %all-gather.3.cloned.1.call-update) | async-done | bytes 6291472 | tf_op jit(solution)/shard_map/all_gather | solution.py:23
  82.2 7.6 %fusion.25 = bf16[96,8,24,128]{3,1,2,0:T(8,128)(2,1)S(1)} fusion(bf16[768,1024]{1,0:T(8,128)(2,1)} %get-tuple-element.12, bf16[1024,3072]{1,0:T(8,128)(2,1)} %all-gather.3.cloned.1.call-done), kind=kOutput, calls=%fused_computation.33 | convolution fusion | flops 4834197504 | bytes 12582912 | tf_op jit(solution)/shard_map/dot_general | solution.py:21
  89.8 1.4 copy.80
  91.2 2.5 fusion.43
  93.7 1.4 copy.100
  95.1 6.5 %all-to-all-start = ((bf16[3,256,8,128]{3,2,0,1:T(8,128)(2,1)}), bf16[3,256,8,128]{3,2,0,1:T(8,128)(2,1)}, u32[]{:S(2)}, u32[]{:S(2)}) async-start(bf16[3,256,8,128]{3,2,0,1:T(8,128)(2,1)} %bitcast.86), calls=%async_computation | async-start | bytes 3145728 | tf_op jit(solution)/shard_map/all_to_all | solution.py:67
  101.6 2.8 copy.99
  104.4 36.4 %all-to-all-done = bf16[3,256,8,128]{3,2,0,1:T(8,128)(2,1)} async-done(((bf16[3,256,8,128]{3,2,0,1:T(8,128)(2,1)}), bf16[3,256,8,128]{3,2,0,1:T(8,128)(2,1)}, u32[]{:S(2)}, u32[]{:S(2)}) %all-to-all-start) | async-done | bytes 1572896 | tf_op jit(solution)/shard_map/all_to_all | solution.py:67
  140.8 4.7 %all-to-all-start.1 = ((bf16[3,256,8,128]{3,2,0,1:T(8,128)(2,1)}), bf16[3,256,8,128]{3,2,0,1:T(8,128)(2,1)}, u32[]{:S(2)}, u32[]{:S(2)}) async-start(bf16[3,256,8,128]{3,2,0,1:T(8,128)(2,1)} %bitcast.85), calls=%async_computation.1 | async-start | bytes 3145728 | tf_op jit(solution)/shard_map/all_to_all | solution.py:65
  145.5 2.8 copy.98
  148.4 36.4 %all-to-all-done.1 = bf16[3,256,8,128]{3,2,0,1:T(8,128)(2,1)} async-done(((bf16[3,256,8,128]{3,2,0,1:T(8,128)(2,1)}), bf16[3,256,8,128]{3,2,0,1:T(8,128)(2,1)}, u32[]{:S(2)}, u32[]{:S(2)}) %all-to-all-start.1) | async-done | bytes 1572896 | tf_op jit(solution)/shard_map/all_to_all | solution.py:65
  184.8 4.7 %all-to-all-start.2 = ((bf16[3,256,8,128]{3,2,0,1:T(8,128)(2,1)}), bf16[3,256,8,128]{3,2,0,1:T(8,128)(2,1)}, u32[]{:S(2)}, u32[]{:S(2)}) async-start(bf16[3,256,8,128]{3,2,0,1:T(8,128)(2,1)} %bitcast.84), calls=%async_computation.2 | async-start | bytes 3145728 | tf_op jit(solution)/shard_map/all_to_all | solution.py:66
  189.5 0.2 all-gather.5.cloned.1.call-start
  189.7 0.5 all-gather.5.cloned.1.call-update
  190.2 9.1 %convolution_convert_fusion = bf16[768,3072]{1,0:T(8,128)(2,1)} fusion(bf16[768,1024]{1,0:T(8,128)(2,1)} %get-tuple-element.11, bf16[1024,3072]{1,0:T(8,128)(2,1)} %param.12), kind=kOutput, calls=%fused_computation.12 | convolution fusion | flops 4834197504 | bytes 12582912 | tf_op jit(solution)/shard_map/dot_general | solution.py:71
  199.3 12.3 %reshape.82 = bf16[3,256,3,16,64]{4,3,2,1,0:T(8,128)(2,1)} reshape(bf16[768,3072]{1,0:T(8,128)(2,1)} %convolution_convert_fusion) | data formatting | bytes 9437184 | tf_op jit(solution)/shard_map/reshape | solution.py:74
  211.6 6.9 %fusion.42 = (bf16[3,256,1,16,64]{4,3,2,1,0:T(8,128)(2,1)}, bf16[3,256,1,16,64]{4,3,2,1,0:T(8,128)(2,1)}, bf16[3,256,1,16,64]{4,3,2,1,0:T(8,128)(2,1)}) fusion(bf16[3,256,3,16,64]{4,3,2,1,0:T(8,128)(2,1)} %reshape.82), kind=kLoop, calls=%fused_computation.51 | loop fusion | bytes 9437184 | tf_op jit(solution)/shard_map/slice | solution.py:86
  218.5 5.0 %copy.77 = bf16[3,256,1,16,64]{1,4,3,0,2:T(8,128)(2,1)} copy(bf16[3,256,1,16,64]{4,3,2,1,0:T(8,128)(2,1)} %get-tuple-element.5) | data formatting | bytes 3145728
  223.5 5.0 %copy.78 = bf16[3,256,1,16,64]{1,4,3,0,2:T(8,128)(2,1)} copy(bf16[3,256,1,16,64]{4,3,2,1,0:T(8,128)(2,1)} %get-tuple-element.6) | data formatting | bytes 3145728
  228.5 5.0 %copy.79 = bf16[3,256,1,16,64]{1,4,3,0,2:T(8,128)(2,1)} copy(bf16[3,256,1,16,64]{4,3,2,1,0:T(8,128)(2,1)} %get-tuple-element.7) | data formatting | bytes 3145728
  233.4 8.2 %fusion.33 = f32[3,16,256,256]{2,3,1,0:T(8,128)} fusion(bf16[3,256,1,16,64]{1,4,3,0,2:T(8,128)(2,1)} %copy.79, bf16[3,256,1,16,64]{1,4,3,0,2:T(8,128)(2,1)} %copy.78), kind=kOutput, calls=%fused_computation.42 | convolution fusion | flops 402653184 | bytes 15728640 | tf_op jit(solution)/shard_map/fphd,fqhd->fhpq/dot_general | solution.py:76
  241.7 2.9 copy.48
  244.6 6.5 %reshape.73 = bf16[96,8,8,2,64]{4,3,2,1,0:T(2,128)(2,1)} reshape(bf16[32,3,8,8,128]{4,3,2,1,0:T(8,128)(2,1)} %copy.48) | data formatting | bytes 3145728 | tf_op jit(solution)/shard_map/reshape | solution.py:45
  251.1 2.9 copy.51
  254.0 6.5 %reshape.74 = bf16[96,8,8,2,64]{4,3,2,1,0:T(2,128)(2,1)} reshape(bf16[32,3,8,8,128]{4,3,2,1,0:T(8,128)(2,1)} %copy.51) | data formatting | bytes 3145728 | tf_op jit(solution)/shard_map/reshape | solution.py:43
  260.5 0.0 all-to-all-done.2
  260.5 2.9 copy.54
  263.5 6.5 %reshape.75 = bf16[96,8,8,2,64]{4,3,2,1,0:T(2,128)(2,1)} reshape(bf16[32,3,8,8,128]{4,3,2,1,0:T(8,128)(2,1)} %copy.54) | data formatting | bytes 3145728 | tf_op jit(solution)/shard_map/reshape | solution.py:44
  269.9 6.8 %fusion.21 = f32[8,8,2,96,96]{3,4,2,1,0:T(8,128)S(1)} fusion(bf16[96,8,8,2,64]{4,3,2,1,0:T(2,128)(2,1)} %reshape.75, bf16[96,8,8,2,64]{4,3,2,1,0:T(2,128)(2,1)} %reshape.74), kind=kOutput, calls=%fused_computation.29 | convolution fusion | flops 150994944 | bytes 7864320 | tf_op jit(solution)/shard_map/fpgjd,epgjd->pgjfe/dot_general | solution.py:47
  276.7 7.5 %fusion.44 = (f32[8,8,2,96]{3,2,1,0:T(2,128)S(1)}, f32[8,8,2,96,96]{3,4,2,1,0:T(8,128)S(1)}) fusion(f32[8,8,2,96,96]{3,4,2,1,0:T(8,128)S(1)} %fusion.21), kind=kOutput, calls=%fused_computation.53 | output fusion | flops 4718687 | bytes 9486336 | tf_op jit(solution)/shard_map/sub | solution.py:50
  284.2 3.9 %fusion.26 = bf16[8,8,2,64,96]{4,3,2,1,0:T(8,128)(2,1)} fusion(f32[8,8,2,96,96]{3,4,2,1,0:T(8,128)S(1)} %get-tuple-element.14, f32[8,8,2,96]{3,2,1,0:T(2,128)S(1)} %get-tuple-element.13, bf16[96,8,8,2,64]{4,3,2,1,0:T(2,128)(2,1)S(1)} %copy-done.2), kind=kOutput, calls=%fused_computation.34 | convolution fusion | flops 154140672 | bytes 7913472 | tf_op jit(solution)/shard_map/pgjfe,epgjd->fpgjd/dot_general | solution.py:51
  288.1 3.9 %copy.59 = bf16[96,8,8,128]{3,2,1,0:T(8,128)(2,1)} copy(bf16[96,8,8,128]{0,3,2,1:T(8,128)(2,1)} %bitcast.87) | data formatting | bytes 3145728 | tf_op jit(solution)/shard_map/reshape | solution.py:54
  292.0 8.7 %all-to-all-start.3 = ((bf16[96,8,8,128]{3,2,1,0:T(8,128)(2,1)}), bf16[96,8,8,128]{3,2,1,0:T(8,128)(2,1)}, u32[]{:S(2)}, u32[]{:S(2)}) async-start(bf16[96,8,8,128]{3,2,1,0:T(8,128)(2,1)} %copy.59), calls=%async_computation.3 | async-start | bytes 3145728 | tf_op jit(solution)/shard_map/all_to_all | solution.py:69
  300.7 15.9 %fusion.45 = (f32[3,16,256]{2,1,0:T(8,128)S(1)}, f32[3,16,256,256]{2,3,1,0:T(8,128)}) fusion(f32[3,16,256,256]{2,3,1,0:T(8,128)} %fusion.33), kind=kOutput, calls=%fused_computation.54 | output fusion | flops 12583167 | bytes 25214976 | tf_op jit(solution)/shard_map/sub | solution.py:84
  316.6 0.0 copy-done.4
  316.6 5.9 %fusion.37 = bf16[3,256,16,64]{1,3,2,0:T(8,128)(2,1)S(1)} fusion(f32[3,16,256,256]{2,3,1,0:T(8,128)} %get-tuple-element.16, f32[3,16,256]{2,1,0:T(8,128)S(1)} %get-tuple-element.15, bf16[3,256,1,16,64]{1,4,3,0,2:T(8,128)(2,1)S(1)} %copy-done.4), kind=kOutput, calls=%fused_computation.46 | convolution fusion | flops 409731072 | bytes 15777792 | tf_op jit(solution)/shard_map/fhpq,fqhd->fphd/dot_general | solution.py:85
  322.5 1.4 copy.66
  323.8 1.5 copy.82
  325.4 14.3 %all-to-all-done.3 = bf16[96,8,8,128]{3,2,1,0:T(8,128)(2,1)} async-done(((bf16[96,8,8,128]{3,2,1,0:T(8,128)(2,1)}), bf16[96,8,8,128]{3,2,1,0:T(8,128)(2,1)}, u32[]{:S(2)}, u32[]{:S(2)}) %all-to-all-start.3) | async-done | bytes 1572896 | tf_op jit(solution)/shard_map/all_to_all | solution.py:69
  339.6 2.7 copy.60
  342.3 4.0 %fusion.30 = f32[768,1024]{1,0:T(8,128)S(1)} fusion(bf16[1024,1024]{1,0:T(8,128)(2,1)} %all-gather.5.cloned.1.call-done, bf16[96,8,8,128]{3,2,1,0:T(8,128)(2,1)} %bitcast.89), kind=kOutput, calls=%fused_computation.36 | convolution fusion | flops 1610612736 | bytes 6815744 | tf_op jit(solution)/shard_map/dot_general | solution.py:31
  346.4 3.2 fusion.18
  (17 shorter events, 0.1 us)
Async XLA Ops:
  6.5 339.8 %copy-start = (bf16[1024,1024]{1,0:T(8,128)(2,1)S(1)}, bf16[1024,1024]{1,0:T(8,128)(2,1)}, u32[]{:S(2)}) copy-start(bf16[1024,1024]{1,0:T(8,128)(2,1)} %param.13) | copy-start | bytes 6291460
  6.5 4.4 %copy-start.5 = (f32[1024]{0:T(1024)S(1)}, f32[1024]{0:T(1024)}, u32[]{:S(2)}) copy-start(f32[1024]{0:T(1024)} %param.9) | copy-start | bytes 12292
  6.5 4.4 %copy-start.6 = (f32[1024]{0:T(1024)S(1)}, f32[1024]{0:T(1024)}, u32[]{:S(2)}) copy-start(f32[1024]{0:T(1024)} %param.8) | copy-start | bytes 12292
  6.5 75.7 %all-gather.3.cloned.1.call-start = ((), (), s32[]{:S(2)}) async-start(), calls=%async_computation.4 | async-start | bytes 6488064 | tf_op jit(solution)/shard_map/all_gather | solution.py:23
  95.1 45.7 %all-to-all-start = ((bf16[3,256,8,128]{3,2,0,1:T(8,128)(2,1)}), bf16[3,256,8,128]{3,2,0,1:T(8,128)(2,1)}, u32[]{:S(2)}, u32[]{:S(2)}) async-start(bf16[3,256,8,128]{3,2,0,1:T(8,128)(2,1)} %bitcast.86), calls=%async_computation | async-start | bytes 3145728 | tf_op jit(solution)/shard_map/all_to_all | solution.py:67
  140.8 43.9 %all-to-all-start.1 = ((bf16[3,256,8,128]{3,2,0,1:T(8,128)(2,1)}), bf16[3,256,8,128]{3,2,0,1:T(8,128)(2,1)}, u32[]{:S(2)}, u32[]{:S(2)}) async-start(bf16[3,256,8,128]{3,2,0,1:T(8,128)(2,1)} %bitcast.85), calls=%async_computation.1 | async-start | bytes 3145728 | tf_op jit(solution)/shard_map/all_to_all | solution.py:65
  184.8 75.7 %all-to-all-start.2 = ((bf16[3,256,8,128]{3,2,0,1:T(8,128)(2,1)}), bf16[3,256,8,128]{3,2,0,1:T(8,128)(2,1)}, u32[]{:S(2)}, u32[]{:S(2)}) async-start(bf16[3,256,8,128]{3,2,0,1:T(8,128)(2,1)} %bitcast.84), calls=%async_computation.2 | async-start | bytes 3145728 | tf_op jit(solution)/shard_map/all_to_all | solution.py:66
  189.5 152.9 %all-gather.5.cloned.1.call-start = ((), (), s32[]{:S(2)}) async-start(), calls=%async_computation.5 | async-start | bytes 2162688 | tf_op jit(solution)/shard_map/all_gather | solution.py:33
  276.7 7.6 %copy-start.2 = (bf16[96,8,8,2,64]{4,3,2,1,0:T(2,128)(2,1)S(1)}, bf16[96,8,8,2,64]{4,3,2,1,0:T(2,128)(2,1)}, u32[]{:S(2)}) copy-start(bf16[96,8,8,2,64]{4,3,2,1,0:T(2,128)(2,1)} %reshape.73) | copy-start | bytes 4718596
  292.0 47.6 %all-to-all-start.3 = ((bf16[96,8,8,128]{3,2,1,0:T(8,128)(2,1)}), bf16[96,8,8,128]{3,2,1,0:T(8,128)(2,1)}, u32[]{:S(2)}, u32[]{:S(2)}) async-start(bf16[96,8,8,128]{3,2,1,0:T(8,128)(2,1)} %copy.59), calls=%async_computation.3 | async-start | bytes 3145728 | tf_op jit(solution)/shard_map/all_to_all | solution.py:69
  300.7 15.9 %copy-start.4 = (bf16[3,256,1,16,64]{1,4,3,0,2:T(8,128)(2,1)S(1)}, bf16[3,256,1,16,64]{1,4,3,0,2:T(8,128)(2,1)}, u32[]{:S(2)}) copy-start(bf16[3,256,1,16,64]{1,4,3,0,2:T(8,128)(2,1)} %copy.77) | copy-start | bytes 4718596
  342.3 4.0 %copy-start.1 = (bf16[3,256,1024]{2,1,0:T(8,128)(2,1)S(1)}, bf16[3,256,1024]{2,1,0:T(8,128)(2,1)}, u32[]{:S(2)}) copy-start(bf16[3,256,1024]{2,1,0:T(8,128)(2,1)} %param.7) | copy-start | bytes 4718596
  342.3 4.0 %copy-start.3 = (bf16[128,8,3,256]{3,1,2,0:T(8,128)(2,1)S(1)}, bf16[128,8,3,256]{3,1,2,0:T(8,128)(2,1)}, u32[]{:S(2)}) copy-start(bf16[128,8,3,256]{3,1,2,0:T(8,128)(2,1)} %copy.82) | copy-start | bytes 4718596
Sparse Core Ops, SparseCore 0:
  9.2 72.9 all-gather.2
  192.2 71.6 all-gather.4
where the time goes:
time: 359 us; the launch traced here: 356 us
  waiting for transfers between devices  156 us (43%)
  local copies, waits for them, and re-layouts  82.8 us (23%)
  matrix products  48.6 us (14%)
  other arithmetic  30.9 us (9%)
  starting transfers between devices  24.7 us (7%)
  between operations  13.6 us (4%)
    all_gather x1, waiting for transfers between devices, time_project(): lax.all_gather(w_tqkv, 'tm', axis=0, tiled=True)  67.5 us
    all_to_all x1, waiting for transfers between devices, body(): lax.all_to_all(queries, 'tm', split_axis=1, concat_axis=0, tiled=True)  36.4 us
    all_to_all x1, waiting for transfers between devices, body(): lax.all_to_all(values_all, 'tm', split_axis=1, concat_axis=0, tiled=True)  36.4 us
    unnamed x22, local copies, waits for them, and re-layouts  24.9 us
    sub x1, other arithmetic, body(): weights = jax.nn.softmax(scores, axis=-1).astype(jnp.bfloat16)  15.9 us
    all_to_all x1, waiting for transfers between devices, body(): lax.all_to_all(mixed, 'tm', split_axis=0, concat_axis=1, tiled=True)  14.3 us
    reshape x1, local copies, waits for them, and re-layouts, body(): space_qkv = space_qkv.reshape(frame_count, patch_count, 3, HEADS, HEAD)  12.3 us
    dot_general x1, matrix products, body(): jnp.dot(normed_space, w_sqkv, preferred_element_type=jnp.float32)  9.07 us
  transfers between devices with their start and end apart: 6, of which 4 were waited for; matrix products, arithmetic and copies ran while one was open for 40% of the time, Pallas kernels for 0%

commit v1 on v0

v1 whole, which is shorter than its diff:
```python
import functools
import math

import jax
import jax.numpy as jnp
from jax import lax
from jax.experimental import pallas as pl
from jax.experimental.pallas import tpu as pltpu
from jax.sharding import PartitionSpec as P

MESH = pl.DeviceIdType.MESH
D = 1024
FRAMES = 3
CHIPS = 16
BLOCK = 16
GROUPS = 4
PAIR = 128
EXP2_SCALE = 0.125 * math.log2(math.e)
F32 = jnp.float32
BF16 = jnp.bfloat16


def dot(a, b):
    return jnp.dot(a, b, preferred_element_type=F32)


def attend_pair(q, k, v):
    n = q.shape[0]
    low = lax.broadcasted_iota(jnp.int32, q.shape, 1) < PAIR // 2
    zero = jnp.zeros_like(q)
    stacked = jnp.concatenate([jnp.where(low, q, zero), jnp.where(low, zero, q)], axis=0).astype(BF16)
    s = lax.dot_general(stacked, k, (((1,), (1,)), ((), ())), preferred_element_type=F32)
    e = jnp.exp2((s - jnp.max(s, axis=-1, keepdims=True)) * EXP2_SCALE)
    p = (e * (1.0 / jnp.sum(e, axis=-1, keepdims=True))).astype(BF16)
    o = dot(p, v)
    return jnp.where(low, o[:n], o[n:])


def kernel(
    x_hbm, gt_ref, gs_ref, wt_hbm, wto_hbm, ws_hbm, wso_hbm, out_hbm,
    xv, nt, ns, tok, ws, wso, wst, cb, wt, wo, acc, mixs, qkvf, mixf, sb, eb, ret, ob,
    ld, sib, fsend, frecv, csend, crecv, zsend, zrecv, ysend, yrecv, losend, lorecv,
    hisend, hirecv, wsend, wrecv, wloc, esend, erecv, rsend, rrecv, outsem,
):
    tm = lax.axis_index("tm")
    cl = lax.axis_index("clip")
    core = tm % 2
    chip = tm // 2
    xl = chip // 8
    z = chip % 8
    y = cl // 2
    xh = cl % 2

    def chip_by(k, sign):
        dx = 1 - k % 2
        m = k // 2
        dz = 4 + (1 - 2 * (m % 2)) * ((m + 1) // 2)
        return (xl + dx - 2 * dx * xl) * 8 + (z + sign * dz + 8) % 8

    def remote(src, dst, s, r, to):
        return pltpu.make_async_remote_copy(
            src_ref=src, dst_ref=dst, send_sem=s, recv_sem=r, device_id=to, device_id_type=MESH
        )

    sibling = (chip * 2 + 1 - core, cl)
    lo_peer = (((1 - xl) * 8 + z) * 2 + core, cl)
    hi_peer = (((1 - xl) * 8 + z) * 2 + core, y * 2 + 1 - xh)

    def y_peer(d):
        return (tm, ((y + d) % 4) * 2 + xh)

    def cols(kind, half):
        return pl.ds(pl.multiple_of(kind * D + half * 512 + y * PAIR, PAIR), PAIR)

    load_x = pltpu.make_async_copy(x_hbm, xv, ld.at[0])
    load_w = []
    for t in range(4):
        src, kind = (wt_hbm, t) if t < 3 else (wto_hbm, 0)
        part = pl.ds(t * PAIR, PAIR)
        load_w.append(pltpu.make_async_copy(src.at[:, cols(kind, 1 - core)], wst.at[:, part], ld.at[1 + t]))
        load_w.append(pltpu.make_async_copy(src.at[:, cols(kind, core)], cb.at[core, :, part], ld.at[5 + t]))
    load_ws = pltpu.make_async_copy(ws_hbm, ws, ld.at[9])
    load_wso = pltpu.make_async_copy(wso_hbm, wso, ld.at[10])
    for c in load_w:
        c.start()
    load_x.start()
    load_ws.start()
    load_wso.start()

    barrier = pltpu.get_barrier_semaphore()

    def greet(k, carry):
        pl.semaphore_signal(barrier, inc=1, device_id=(chip_by(k, 1) * 2 + core, cl), device_id_type=MESH)
        return carry

    lax.fori_loop(0, CHIPS - 1, greet, 0)
    for to in (sibling, hi_peer, y_peer(1), y_peer(2), y_peer(3)):
        pl.semaphore_signal(barrier, inc=1, device_id=to, device_id_type=MESH)
    pl.semaphore_wait(barrier, CHIPS + 4)

    for c in load_w:
        c.wait()
    to_sib = remote(wst, cb.at[core], sib.at[0], sib.at[1], sibling)
    to_sib.start()

    gain_t = gt_ref[...]
    gain_s = gs_ref[...]

    def norm(target):
        for f in range(FRAMES):
            v = xv[f, target].astype(F32)
            c = v - jnp.mean(v, axis=-1, keepdims=True)
            n = c * lax.rsqrt(jnp.mean(c * c, axis=-1, keepdims=True) + 1e-5)
            nt[f, target] = (n * gain_t).astype(BF16)
            ns[f, target] = (n * gain_s).astype(BF16)

    load_x.wait()
    norm(chip)

    to_sib.wait_recv()

    def z_copy(d):
        to = ((xl * 8 + (z + d) % 8) * 2 + core, cl)
        return remote(cb, wt.at[y, chip], zsend.at[d - 1], zrecv.at[d - 1], to)

    def z_start(i, carry):
        z_copy(i).start()
        return carry

    lax.fori_loop(1, 8, z_start, 0)
    own_w = pltpu.make_async_copy(cb, wt.at[y, chip], wloc.at[4])
    own_w.start()

    def tok_copy(k):
        to = chip_by(k, 1)
        return remote(nt.at[:, to], tok.at[chip, core], fsend.at[k], frecv.at[k], (to * 2 + core, cl))

    def tok_start(k, carry):
        norm(chip_by(k, 1))
        tok_copy(k).start()
        return carry

    lax.fori_loop(0, CHIPS - 1, tok_start, 0)
    own_tok = pltpu.make_async_copy(nt.at[:, chip], tok.at[chip, core], wloc.at[5])
    own_tok.start()

    def share_copy(k, src):
        js = chip_by(k, -1)
        return remote(src, tok.at[js, core], csend.at[k], crecv.at[k], sibling)

    share_own = share_copy(CHIPS - 1, nt.at[:, chip])
    share_own.start()

    def space_frame(f):
        def quad(h, carry):
            a = ns[f].reshape(CHIPS * BLOCK, D)
            c0 = pl.multiple_of(h * 256, 256)
            q = dot(a, ws[:, pl.ds(c0, 256)])
            k = dot(a, ws[:, pl.ds(c0 + D, 256)]).astype(BF16)
            v = dot(a, ws[:, pl.ds(c0 + 2 * D, 256)]).astype(BF16)
            for i in range(2):
                part = slice(i * PAIR, (i + 1) * PAIR)
                o = attend_pair(q[:, part], k[:, part], v[:, part])
                mixs[:, pl.ds(pl.multiple_of(c0 + i * PAIR, PAIR), PAIR)] = o.astype(BF16)
            return carry

        lax.fori_loop(0, 4, quad, 0)

        def project(h, carry):
            c = pl.ds(pl.multiple_of(h * 256, 256), 256)
            xs = xv[f, :, :, c].reshape(CHIPS * BLOCK, 256).astype(F32)
            acc[f, :, c] = xs + dot(mixs[...], wso[:, c])
            return carry

        lax.fori_loop(0, 4, project, 0)

    def y_copy(d):
        part = wt.at[y, pl.ds(xl * 8, 8)]
        return remote(part, part, ysend.at[d - 1], yrecv.at[d - 1], y_peer(d))

    def x_copies(d):
        g = (y + 4 - d) % 4
        lo = wt.at[g, pl.ds(xl * 8, 3)]
        hi = wt.at[g, pl.ds(xl * 8 + 3, 5)]
        return (
            remote(lo, lo, losend.at[d], lorecv.at[d], lo_peer),
            remote(hi, hi, hisend.at[d], hirecv.at[d], hi_peer),
        )

    def x_start(d):
        for c in x_copies(d):
            c.start()

    load_ws.wait()
    load_wso.wait()
    space_frame(0)

    def z_wait(i, carry):
        z_copy(i).wait_recv()
        return carry

    lax.fori_loop(1, 8, z_wait, 0)
    own_w.wait()
    for d in (1, 3, 2):
        y_copy(d).start()
    x_start(0)
    space_frame(1)
    for d in (1, 3):
        y_copy(d).wait_recv()
        x_start(d)
    space_frame(2)
    y_copy(2).wait_recv()
    x_start(2)

    def tok_share(k, carry):
        tok_copy(k).wait_recv()
        share_copy(k, tok.at[chip_by(k, -1), core]).start()
        return carry

    lax.fori_loop(0, CHIPS - 1, tok_share, 0)
    own_tok.wait()

    for d in range(4):
        for c in x_copies(d):
            c.wait_recv()

    def wo_copies(g):
        src = wt.at[g, :, :, :, pl.ds(3 * PAIR, PAIR)]
        dst = wo.at[:, :, :, pl.ds(pl.multiple_of(core * 512 + g * PAIR, PAIR), PAIR)]
        return (
            pltpu.make_async_copy(src, dst, wloc.at[g]),
            remote(src, dst, wsend.at[g], wrecv.at[g], sibling),
        )

    for g in range(GROUPS):
        for c in wo_copies(g):
            c.start()

    def share_wait(k, carry):
        share_copy(k, tok.at[chip_by(k, -1), core]).wait_recv()
        return carry

    lax.fori_loop(0, CHIPS, share_wait, 0)

    def eb_copy(g):
        dst = sb.at[g, :, :, :, pl.ds(pl.multiple_of(core * PAIR, PAIR), PAIR)]
        return remote(eb.at[g], dst, esend.at[g], erecv.at[g], sibling)

    def ret_copy(g, k):
        to = chip_by(k, 1)
        return remote(sb.at[g, to], ret.at[g, :, chip], rsend.at[g, k], rrecv.at[g, k], (to * 2 + core, cl))

    def time_group(g, carry):
        def project(mb, carry):
            a = tok[pl.ds(mb * 4, 4)].reshape(384, D)
            w = wt[g, :, :, :, : 3 * PAIR].reshape(D, 3 * PAIR)
            qkv = dot(a, w)
            for t in range(3):
                qkvf[t, pl.ds(pl.multiple_of(mb * 384, 384), 384), :] = qkv[:, t * PAIR : (t + 1) * PAIR]
            return carry

        lax.fori_loop(0, 4, project, 0)

        def patches(i, carry):
            for u in range(4):
                rows = pl.ds(i * 4 + u, 96, stride=BLOCK)
                q = qkvf[0, rows, :]
                k = qkvf[1, rows, :].astype(BF16)
                v = qkvf[2, rows, :].astype(BF16)
                mixf[rows, :] = attend_pair(q, k, v)
            return carry

        lax.fori_loop(0, BLOCK // 4, patches, 0)

        def settle(j, carry):
            mine = pl.ds(pl.multiple_of(j * 96 + core * 48, 16), 48)
            other = pl.ds(pl.multiple_of(j * 96 + (1 - core) * 48, 16), 48)
            here = pl.ds(pl.multiple_of(core * PAIR, PAIR), PAIR)
            sb[g, j, :, :, here] = mixf[mine, :].astype(BF16).reshape(FRAMES, BLOCK, PAIR)
            eb[g, j] = mixf[other, :].astype(BF16).reshape(FRAMES, BLOCK, PAIR)
            return carry

        lax.fori_loop(0, CHIPS, settle, 0)
        eb_copy(g).start()
        eb_copy(g).wait_recv()

        def ret_start(k, carry):
            ret_copy(g, k).start()
            return carry

        lax.fori_loop(0, CHIPS - 1, ret_start, 0)
        ret[g, :, chip] = sb[g, chip]
        return carry

    lax.fori_loop(0, GROUPS, time_group, 0)

    for g in range(GROUPS):
        here, there = wo_copies(g)
        here.wait()
        there.wait_recv()

    def final(g, last):
        def ret_wait(k, carry):
            ret_copy(g, k).wait_recv()
            return carry

        lax.fori_loop(0, CHIPS - 1, ret_wait, 0)

        def project(f, carry):
            a = ret[g, f].reshape(CHIPS * BLOCK, 256)
            for h in range(2):
                c = pl.ds(h * 512, 512)
                w = jnp.concatenate(
                    [
                        wo[pl.ds(2 * g, 2), :, :, c].reshape(PAIR, 512),
                        wo[pl.ds(8 + 2 * g, 2), :, :, c].reshape(PAIR, 512),
                    ],
                    axis=0,
                )
                total = acc[f, :, c] + dot(a, w)
                if last:
                    ob[f, :, c] = total.astype(BF16)
                else:
                    acc[f, :, c] = total
            if last:
                pltpu.make_async_copy(ob.at[f], out_hbm.at[f], outsem.at[f]).start()
            return carry

        lax.fori_loop(0, FRAMES, project, 0)

    def final_step(g, carry):
        final(g, False)
        return carry

    lax.fori_loop(0, GROUPS - 1, final_step, 0)
    final(GROUPS - 1, True)

    to_sib.wait_send()

    def z_sent(i, carry):
        z_copy(i).wait_send()
        return carry

    lax.fori_loop(1, 8, z_sent, 0)
    for d in (1, 3, 2):
        y_copy(d).wait_send()
    for d in range(4):
        for c in x_copies(d):
            c.wait_send()
    for g in range(GROUPS):
        wo_copies(g)[1].wait_send()

    def tok_sent(k, carry):
        tok_copy(k).wait_send()
        return carry

    lax.fori_loop(0, CHIPS - 1, tok_sent, 0)

    def share_sent(k, carry):
        share_copy(k, tok.at[chip_by(k, -1), core]).wait_send()
        return carry

    lax.fori_loop(0, CHIPS, share_sent, 0)

    def ret_sent(i, carry):
        g = i // 15
        ret_copy(g, i % 15).wait_send()
        return carry

    lax.fori_loop(0, GROUPS * (CHIPS - 1), ret_sent, 0)

    def eb_sent(g, carry):
        eb_copy(g).wait_send()
        return carry

    lax.fori_loop(0, GROUPS, eb_sent, 0)
    for f in range(FRAMES):
        pltpu.make_async_copy(ob.at[f], out_hbm.at[f], outsem.at[f]).wait()


def body(frames_in, gain_time, gain_space, w_tqkv, w_tout, w_sqkv, w_sout):
    dma = pltpu.SemaphoreType.DMA
    vmem = pl.BlockSpec(memory_space=pltpu.VMEM)
    hbm = pl.BlockSpec(memory_space=pl.ANY)
    out = pl.pallas_call(
        kernel,
        out_shape=jax.ShapeDtypeStruct((FRAMES, CHIPS * BLOCK, D), BF16),
        in_specs=[hbm, vmem, vmem, hbm, hbm, hbm, hbm],
        out_specs=hbm,
        scratch_shapes=[
            pltpu.VMEM((FRAMES, CHIPS, BLOCK, D), BF16),
            pltpu.VMEM((FRAMES, CHIPS, BLOCK, D), BF16),
            pltpu.VMEM((FRAMES, CHIPS, BLOCK, D), BF16),
            pltpu.VMEM((CHIPS, 2, FRAMES, BLOCK, D), BF16),
            pltpu.VMEM((D, 3 * D), BF16),
            pltpu.VMEM((D, D), BF16),
            pltpu.VMEM((32, 512), BF16),
            pltpu.VMEM((2, 32, 512), BF16),
            pltpu.VMEM((GROUPS, CHIPS, 2, 32, 512), BF16),
            pltpu.VMEM((CHIPS, 2, 32, D), BF16),
            pltpu.VMEM((FRAMES, CHIPS * BLOCK, D), F32),
            pltpu.VMEM((CHIPS * BLOCK, D), BF16),
            pltpu.VMEM((3, CHIPS * 96, PAIR), F32),
            pltpu.VMEM((CHIPS * 96, PAIR), F32),
            pltpu.VMEM((GROUPS, CHIPS, FRAMES, BLOCK, 2 * PAIR), BF16),
            pltpu.VMEM((GROUPS, CHIPS, FRAMES, BLOCK, PAIR), BF16),
            pltpu.VMEM((GROUPS, FRAMES, CHIPS, BLOCK, 2 * PAIR), BF16),
            pltpu.VMEM((FRAMES, CHIPS * BLOCK, D), BF16),
            dma((11,)),
            dma((2,)),
            dma((15,)), dma((15,)),
            dma((16,)), dma((16,)),
            dma((7,)), dma((7,)),
            dma((3,)), dma((3,)),
            dma((4,)), dma((4,)),
            dma((4,)), dma((4,)),
            dma((4,)), dma((4,)),
            dma((6,)),
            dma((4,)), dma((4,)),
            dma((4, 15)), dma((4, 15)),
            dma((3,)),
        ],
        compiler_params=pltpu.CompilerParams(
            collective_id=0, has_side_effects=True, vmem_limit_bytes=56 * 2**20
        ),
        name="encoder_block",
    )(
        frames_in.reshape(FRAMES, CHIPS, BLOCK, D),
        gain_time.reshape(1, D),
        gain_space.reshape(1, D),
        w_tqkv, w_tout, w_sqkv, w_sout,
    )
    return out


def solution(mesh):
    in_specs = (P(("clip", "tm"), None, None), P(), P(), P("tm", None), P("tm", None), P(), P())
    out_specs = P(("clip", "tm"), None, None)
    return jax.shard_map(body, mesh=mesh, in_specs=in_specs, out_specs=out_specs, check_vma=False)
```

time: 359 us -> 119 us (0.33)
  waiting for transfers between devices: 156 us -> 0 us
  Pallas kernels: 0 us -> 116 us
  local copies, waits for them, and re-layouts: 82.8 us -> 2.67 us
  matrix products: 48.6 us -> 0 us
  other arithmetic: 30.9 us -> 0 us
  starting transfers between devices: 24.7 us -> 0 us
  between operations: 13.6 us -> 0.01 us
    pallas_call x0 -> x1, Pallas kernels: none -> 116 us  [body(): pl.pallas_call(kernel, out_shape=jax.ShapeDtypeStruct((FRAMES, CHIPS * BL...]
    all_to_all x4 -> x0, waiting for transfers between devices: 87.1 us -> none  [the longest x1 36.4 us: body(): lax.all_to_all(queries, 'tm', split_axis=1, concat_axis=0, tiled=True)]
    all_gather x2 -> x0, waiting for transfers between devices: 67.5 us -> none  [the longest x1 67.5 us: time_project(): lax.all_gather(w_tqkv, 'tm', axis=0, tiled=True)]
    dot_general x8 -> x0, matrix products: 48.6 us -> none  [the longest x1 9.07 us: body(): jnp.dot(normed_space, w_sqkv, preferred_element_type=jnp.float32)]
    reshape x5 -> x0, local copies, waits for them, and re-layouts: 35.6 us -> none  [the longest x1 12.3 us: body(): space_qkv = space_qkv.reshape(frame_count, patch_count, 3, HEADS, HEAD)]
    all_to_all x4 -> x0, starting transfers between devices: 24.5 us -> none  [the longest x1 8.67 us: body(): lax.all_to_all(mixed, 'tm', split_axis=0, concat_axis=1, tiled=True)]
    sub x2 -> x0, other arithmetic: 23.4 us -> none  [the longest x1 15.9 us: body(): weights = jax.nn.softmax(scores, axis=-1).astype(jnp.bfloat16)]
    unnamed x22 -> x1, local copies, waits for them, and re-layouts: 24.9 us -> 2.67 us
  transfers between devices with their start and end apart: 6 -> 0, of which waited for: 4 -> 0; matrix products, arithmetic and copies ran while one was open for 40% -> 0% of each run, Pallas kernels for 0% -> 0%
where the time goes in v1:
time: 119 us; the launch traced here: 118 us
  Pallas kernels  116 us (97%)
  local copies, waits for them, and re-layouts  2.67 us (2%)
    pallas_call x1, Pallas kernels, body(): pl.pallas_call(kernel, out_shape=jax.ShapeDtypeStruct((FRAMES, CHIPS * BL...  116 us
    unnamed x1, local copies, waits for them, and re-layouts  2.67 us

profile of v1, /device:TPU:16, one launch (start us, length us, event | category | flops | bytes accessed | tf_op | source)
XLA Modules:
  0.0 118.3 jit_solution(5753780058924323578)
XLA Ops:
  0.0 115.6 %encoder_block.1 = bf16[3,256,1024]{2,1,0:T(8,128)(2,1)} custom-call(bf16[3,16,16,1024]{3,2,1,0:T(8,128)(2,1)} %bitcast.3, f32[1,1024]{1,0:T(1,128)} %bitcast.4, f32[1,1024]{1,0:T(1,128)} %bitcast.5, bf16[32,3072]{1,0:T(8,128)(2,1)} %wt_hbm.1, bf16[32,1024]{1,0:T(8,128)(2,1)} %wto_hbm.1, bf16[1024,3072]{1,0:T(8,128)(2,1)} %ws_hbm.1, bf16[1024,1024]{1,0:T(8,128)(2,1)} %wso_hbm.1), custom_call_target="tpu_custom_call" | custom-call | tf_op jit(solution)/shard_map/encoder_block/pallas_call | solution.py:385
  115.6 2.7 %copy.9 = bf16[3,256,1024]{2,1,0:T(8,128)(2,1)} copy(bf16[3,256,1024]{2,1,0:T(8,128)(2,1)} %encoder_block.1) | data formatting | bytes 3145728

commit v2 on v1

v2 whole, which is shorter than its diff:
```python
import functools
import math

import jax
import jax.numpy as jnp
from jax import lax
from jax.experimental import pallas as pl
from jax.experimental.pallas import tpu as pltpu
from jax.sharding import PartitionSpec as P

MESH = pl.DeviceIdType.MESH
D = 1024
FRAMES = 3
CHIPS = 16
BLOCK = 16
GROUPS = 4
PAIR = 128
Z_ORDER = (1, 7, 2, 6, 3, 5, 4)
WINDOW = 14
IN_TILES = (pl.ds(0, 2), pl.ds(2, 1))
OUT_TILES = (pl.ds(0, 1), pl.ds(1, 2))
EXP2_SCALE = 0.125 * math.log2(math.e)
F32 = jnp.float32
BF16 = jnp.bfloat16


def dot(a, b):
    return jnp.dot(a, b, preferred_element_type=F32)


def attend_pairs(triples):
    n = triples[0][0].shape[0]
    low = lax.broadcasted_iota(jnp.int32, (n, PAIR), 1) < PAIR // 2
    both = jnp.concatenate([low, low], axis=1)
    zero = jnp.zeros((n, PAIR), F32)
    stacked = [
        jnp.concatenate([jnp.where(low, q, zero), jnp.where(low, zero, q)], axis=0).astype(BF16)
        for q, _, _ in triples
    ]
    scores = [
        lax.dot_general(q, k, (((1,), (1,)), ((), ())), preferred_element_type=F32)
        for q, (_, k, _) in zip(stacked, triples)
    ]
    tops = [jnp.max(s, axis=-1, keepdims=True) for s in scores]
    weights = [jnp.exp2((s - m) * EXP2_SCALE).astype(BF16) for s, m in zip(scores, tops)]
    mixed = [
        dot(e, jnp.concatenate([v, jnp.ones_like(v)], axis=1)) for e, (_, _, v) in zip(weights, triples)
    ]
    out = []
    for o in mixed:
        o = jnp.where(both, o[:n], o[n:])
        out.append(o[:, :PAIR] / o[:, PAIR:])
    return out


def kernel(
    x_hbm, gt_ref, gs_ref, wt_hbm, wto_hbm, ws_hbm, wso_hbm, out_hbm,
    xv, nt, ns, tok, ws, wso, wst, cb, wz, wt, wot, wo, acc, mixs, qa, qb, ma, mb, sb, eb, ret, ob,
    ld, sib, fsend, frecv, csend, crecv, zsend, zrecv, ysend, yrecv, losend, lorecv,
    hisend, hirecv, wsend, wrecv, wloc, esend, erecv, rsend, rrecv, outsem,
):
    tm = lax.axis_index("tm")
    cl = lax.axis_index("clip")
    core = tm % 2
    chip = tm // 2
    xl = chip // 8
    z = chip % 8
    y = cl // 2
    xh = cl % 2

    def chip_by(k, sign):
        last = k // 14
        dx = k % 2 + last - 2 * last * (k % 2)
        m = k // 2
        odd = m % 2
        dz = ((1 - odd) * (m // 2 + 1) + odd * (8 - (m + 1) // 2)) * (1 - last)
        return (xl + dx - 2 * dx * xl) * 8 + (z + sign * dz + 8) % 8

    def remote(src, dst, s, r, to):
        return pltpu.make_async_remote_copy(
            src_ref=src, dst_ref=dst, send_sem=s, recv_sem=r, device_id=to, device_id_type=MESH
        )

    sibling = (chip * 2 + 1 - core, cl)
    lo_peer = (((1 - xl) * 8 + z) * 2 + core, cl)
    hi_peer = (((1 - xl) * 8 + z) * 2 + core, y * 2 + 1 - xh)

    def y_peer(d):
        return (tm, ((y + d) % 4) * 2 + xh)

    def cols(kind, half):
        return pl.ds(pl.multiple_of(kind * D + half * 512 + y * PAIR, PAIR), PAIR)

    load_x = pltpu.make_async_copy(x_hbm, xv, ld.at[0])
    load_w = []
    for t in range(4):
        src, kind = (wt_hbm, t) if t < 3 else (wto_hbm, 0)
        part = pl.ds(t * PAIR, PAIR)
        load_w.append(pltpu.make_async_copy(src.at[:, cols(kind, 1 - core)], wst.at[:, part], ld.at[1 + t]))
        load_w.append(pltpu.make_async_copy(src.at[:, cols(kind, core)], cb.at[core, :, part], ld.at[5 + t]))
    load_ws = pltpu.make_async_copy(ws_hbm, ws, ld.at[9])
    load_wso = pltpu.make_async_copy(wso_hbm, wso, ld.at[10])
    load_x.start()
    for c in load_w:
        c.start()
    load_ws.start()
    load_wso.start()

    barrier = pltpu.get_barrier_semaphore()

    def greet(k, carry):
        pl.semaphore_signal(barrier, inc=1, device_id=(chip_by(k, 1) * 2 + core, cl), device_id_type=MESH)
        return carry

    lax.fori_loop(0, CHIPS - 1, greet, 0)
    for to in (sibling, hi_peer, y_peer(1), y_peer(2), y_peer(3)):
        pl.semaphore_signal(barrier, inc=1, device_id=to, device_id_type=MESH)

    gain_t = gt_ref[...]
    gain_s = gs_ref[...]
    load_x.wait()

    def norm(j, carry):
        normed = []
        for f in range(FRAMES):
            v = xv[f, j].astype(F32)
            c = v - jnp.mean(v, axis=-1, keepdims=True)
            n = c * lax.rsqrt(jnp.mean(c * c, axis=-1, keepdims=True) + 1e-5)
            normed.append(n * gain_t)
            ns[f, j] = (n * gain_s).astype(BF16)
        nt[j, 0] = jnp.concatenate([normed[0][:8], normed[1][:8]], axis=0).astype(BF16)
        nt[j, 1] = normed[2].astype(BF16)
        nt[j, 2] = jnp.concatenate([normed[0][8:], normed[1][8:]], axis=0).astype(BF16)
        return carry

    lax.fori_loop(0, CHIPS, norm, 0)
    for c in load_w:
        c.wait()
    pl.semaphore_wait(barrier, CHIPS + 4)

    to_sib = remote(wst, cb.at[core], sib.at[0], sib.at[1], sibling)
    to_sib.start()

    def tok_copy(h, k):
        to = chip_by(k, 1)
        return remote(
            nt.at[to, IN_TILES[h]], tok.at[chip, core, IN_TILES[h]],
            fsend.at[h, k], frecv.at[h, k], (to * 2 + core, cl),
        )

    def tok_start(n, carry):
        h = n // (CHIPS - 1)
        for v in range(2):

            @pl.when(h == v)
            def _():
                tok_copy(v, n - v * (CHIPS - 1)).start()

        return carry

    def tok_sent(n, carry):
        h = n // (CHIPS - 1)
        for v in range(2):

            @pl.when(h == v)
            def _():
                tok_copy(v, n - v * (CHIPS - 1)).wait_send()

        return carry

    def tok_share(h):
        def share(k, carry):
            tok_copy(h, k).wait_recv()
            share_copy(h, k, tok.at[chip_by(k, -1), core]).start()
            return carry

        return share

    def share_copy(h, k, src):
        return remote(
            src.at[IN_TILES[h]], tok.at[chip_by(k, -1), core, IN_TILES[h]],
            csend.at[h, k], crecv.at[h, k], sibling,
        )

    lax.fori_loop(0, 4, tok_start, 0)

    def z_copy(kind, d):
        part = (slice(None), slice(None), pl.ds(0, 3 * PAIR) if kind == 0 else pl.ds(3 * PAIR, PAIR))
        to = ((xl * 8 + (z + d) % 8) * 2 + core, cl)
        return remote(cb.at[part], wz.at[z].at[part], zsend.at[kind, d - 1], zrecv.at[kind, d - 1], to)

    def z_start(kind):
        for d in Z_ORDER:
            z_copy(kind, d).start()

    def z_wait(kind):
        for d in Z_ORDER:
            z_copy(kind, d).wait_recv()

    to_sib.wait_recv()
    z_start(0)
    own_w = pltpu.make_async_copy(cb, wz.at[z], wloc.at[4])
    own_w.start()
    lax.fori_loop(4, WINDOW, tok_start, 0)
    own_tok = pltpu.make_async_copy(nt.at[chip], tok.at[chip, core], wloc.at[5])
    own_tok.start()
    for h in range(2):
        share_copy(h, CHIPS - 1, nt.at[chip]).start()

    def own_part(kind, first, count):
        part = pl.ds(0, 3 * PAIR) if kind == 0 else pl.ds(3 * PAIR, PAIR)
        return wz.at[pl.ds(first, count), :, :, part]

    def held(kind, g, first, count):
        return (wt, wot)[kind].at[g, pl.ds(xl * 8 + first, count)]

    def y_copy(kind, d):
        return remote(
            own_part(kind, 0, 8), held(kind, y, 0, 8),
            ysend.at[kind, d - 1], yrecv.at[kind, d - 1], y_peer(d),
        )

    def x_copies(kind, d):
        g = (y + 4 - d) % 4
        out = []
        for first, count, s, r, to in ((0, 3, losend, lorecv, lo_peer), (3, 5, hisend, hirecv, hi_peer)):
            dst = held(kind, g, first, count)
            src = own_part(kind, first, count) if d == 0 else dst
            out.append(remote(src, dst, s.at[kind, d], r.at[kind, d], to))
        return out

    def x_start(kind, d):
        for c in x_copies(kind, d):
            c.start()

    def y_start(kind):
        for d in (1, 3, 2):
            y_copy(kind, d).start()
        x_start(kind, 0)

    def keep_own(kind):
        return pltpu.make_async_copy(own_part(kind, 0, 8), held(kind, y, 0, 8), wloc.at[6 + kind])

    load_ws.wait()
    load_wso.wait()

    def space(i, carry):
        f = i // 4
        c0 = pl.multiple_of((i % 4) * 256, 256)
        a = ns[f].reshape(CHIPS * BLOCK, D)
        q = dot(a, ws[:, pl.ds(c0, 256)])
        k = dot(a, ws[:, pl.ds(c0 + D, 256)]).astype(BF16)
        v = dot(a, ws[:, pl.ds(c0 + 2 * D, 256)]).astype(BF16)
        parts = [slice(u * PAIR, (u + 1) * PAIR) for u in range(2)]
        for u, o in enumerate(attend_pairs([(q[:, p], k[:, p], v[:, p]) for p in parts])):
            mixs[:, pl.ds(pl.multiple_of(c0 + u * PAIR, PAIR), PAIR)] = o.astype(BF16)

        @pl.when(i % 4 == 3)
        def _():
            def project(h, carry):
                c = pl.ds(pl.multiple_of(h * 256, 256), 256)
                xs = xv[f, :, :, c].reshape(CHIPS * BLOCK, 256).astype(F32)
                acc[f, :, :, :, c] = (xs + dot(mixs[...], wso[:, c])).reshape(CHIPS, 2, 8, 256)
                return carry

            lax.fori_loop(0, 4, project, 0)

        @pl.when(i == 0)
        def _():
            z_wait(0)
            own_w.wait()
            y_start(0)
            keep_own(0).start()

        for u in range(2):
            tok_sent(2 * i + u, 0)

            @pl.when(2 * i + u + WINDOW < 2 * (CHIPS - 1))
            def _():
                tok_start(2 * i + u + WINDOW, 0)

        @pl.when((i >= 2) & (i < 9))
        def _():
            for u in range(2):
                tok_share(0)(2 * i - 4 + u, 0)

        @pl.when(i == 4)
        def _():
            for d in (1, 3):
                y_copy(0, d).wait_recv()
                x_start(0, d)

        @pl.when(i == 7)
        def _():
            y_copy(0, 2).wait_recv()
            x_start(0, 2)

        return carry

    lax.fori_loop(0, 12, space, 0)

    def share_wait(h):
        def wait(k, carry):
            share_copy(h, k, tok.at[chip_by(k, -1), core]).wait_recv()
            return carry

        return wait

    z_start(1)
    tok_share(0)(CHIPS - 2, 0)
    own_tok.wait()
    keep_own(0).wait()
    for d in range(4):
        for c in x_copies(0, d):
            c.wait_recv()
    lax.fori_loop(0, CHIPS, share_wait(0), 0)

    def wo_copies(g):
        dst = wo.at[:, :, :, pl.ds(pl.multiple_of(core * 512 + g * PAIR, PAIR), PAIR)]
        return (
            pltpu.make_async_copy(wot.at[g], dst, wloc.at[g]),
            remote(wot.at[g], dst, wsend.at[g], wrecv.at[g], sibling),
        )

    def eb_copy(h, g):
        dst = sb.at[g, :, OUT_TILES[h], :, pl.ds(pl.multiple_of(core * PAIR, PAIR), PAIR)]
        return remote(eb.at[g, :, OUT_TILES[h]], dst, esend.at[h, g], erecv.at[h, g], sibling)

    def ret_copy(h, g, k):
        to = chip_by(k, 1)
        return remote(
            sb.at[g, to, OUT_TILES[h]], ret.at[g, chip, OUT_TILES[h]],
            rsend.at[h, g, k], rrecv.at[h, g, k], (to * 2 + core, cl),
        )

    def send_back(h, g):
        eb_copy(h, g).wait_recv()

        def ret_start(k, carry):
            ret_copy(h, g, k).start()
            return carry

        lax.fori_loop(0, CHIPS - 1, ret_start, 0)
        ret[g, chip, OUT_TILES[h]] = sb[g, chip, OUT_TILES[h]]

    def attend_patches(qkv, out):
        def patches(i, carry):
            rows = [pl.ds(i * 4 + u, 96, stride=8) for u in range(4)]
            triples = [(qkv(0, r), qkv(1, r).astype(BF16), qkv(2, r).astype(BF16)) for r in rows]
            for r, o in zip(rows, attend_pairs(triples)):
                out[r, :] = o
            return carry

        lax.fori_loop(0, 2, patches, 0)

    here = pl.ds(pl.multiple_of(core * PAIR, PAIR), PAIR)

    def first_group(g, carry):
        def project(n, carry):
            a = tok[pl.ds(n * 8, 8), :, 0:2].reshape(512, D)
            r = dot(a, wt[g].reshape(D, 3 * PAIR))
            for t in range(3):
                part = r[:, t * PAIR : (t + 1) * PAIR]
                for i in range(16):
                    at = pl.multiple_of((n * 16 + i) * 24, 8)
                    qa[t, pl.ds(at, 24), :] = part[i * 32 : i * 32 + 24]
                    qb[g * 3 + t, pl.ds(at, 8), :] = part[i * 32 + 24 : i * 32 + 32]
            return carry

        lax.fori_loop(0, 2, project, 0)

        @pl.when(g > 0)
        def _():
            send_back(0, g - 1)

        attend_patches(lambda t, rows: qa[t, rows, :], ma.at[g])

        def settle(j, carry):
            for mine in range(2):
                at = (j * 2 + (core if mine else 1 - core)) * 24
                tile = ma[g, pl.ds(pl.multiple_of(at, 8), 16), :].astype(BF16)
                if mine:
                    sb[g, j, 0, :, here] = tile
                else:
                    eb[g, j, 0] = tile
            return carry

        lax.fori_loop(0, CHIPS, settle, 0)
        eb_copy(0, g).start()

        @pl.when(g > 0)
        def _():
            lax.fori_loop((g - 1) * 5, g * 5, tok_share(1), 0)

        @pl.when(g == 1)
        def _():
            z_wait(1)
            y_start(1)
            keep_own(1).start()

        return carry

    lax.fori_loop(0, GROUPS, first_group, 0)
    lax.fori_loop(0, CHIPS, share_wait(1), 0)

    def second_group(g, carry):
        def project(n, carry):
            a = tok[pl.ds(n * 8, 8), :, 2].reshape(256, D)
            r = dot(a, wt[g].reshape(D, 3 * PAIR))
            for t in range(3):
                part = r[:, t * PAIR : (t + 1) * PAIR]
                for i in range(16):
                    at = pl.multiple_of((n * 16 + i) * 24 + 8, 8)
                    qb[g * 3 + t, pl.ds(at, 16), :] = part[i * 16 : i * 16 + 16]
            return carry

        lax.fori_loop(0, 2, project, 0)

        @pl.when(g == 0)
        def _():
            send_back(0, GROUPS - 1)

        @pl.when(g > 0)
        def _():
            send_back(1, g - 1)

        attend_patches(lambda t, rows: qb[g * 3 + t, rows, :], mb)

        def settle(j, carry):
            for mine in range(2):
                at = (j * 2 + (core if mine else 1 - core)) * 24
                first = ma[g, pl.ds(pl.multiple_of(at + 16, 8), 8), :]
                rest = mb[pl.ds(pl.multiple_of(at, 8), 24), :]
                one = jnp.concatenate([first, rest[:8]], axis=0).astype(BF16)
                two = rest[8:].astype(BF16)
                if mine:
                    sb[g, j, 1, :, here] = one
                    sb[g, j, 2, :, here] = two
                else:
                    eb[g, j, 1] = one
                    eb[g, j, 2] = two
            return carry

        lax.fori_loop(0, CHIPS, settle, 0)
        eb_copy(1, g).start()

        @pl.when(g == 0)
        def _():
            for d in (1, 3, 2):
                y_copy(1, d).wait_recv()
                x_start(1, d)

        @pl.when(g == 2)
        def _():
            for d in range(4):
                for c in x_copies(1, d):
                    c.wait_recv()
            keep_own(1).wait()
            for n in range(GROUPS):
                for c in wo_copies(n):
                    c.start()

        return carry

    lax.fori_loop(0, GROUPS, second_group, 0)
    send_back(1, GROUPS - 1)

    for g in range(GROUPS):
        here_copy, there_copy = wo_copies(g)
        here_copy.wait()
        there_copy.wait_recv()

    def out_copy(n):
        part = pl.ds(n * 4, 4)
        return pltpu.make_async_copy(ob.at[:, part], out_hbm.at[:, part], outsem.at[n])

    def final(g, last):
        def ret_wait(k, carry):
            ret_copy(0, g, k).wait_recv()
            ret_copy(1, g, k).wait_recv()
            return carry

        lax.fori_loop(0, CHIPS - 1, ret_wait, 0)

        def project(n, carry):
            js = pl.ds(n * 4, 4)
            a = ret[g, js].reshape(192, 256)
            for h in range(2):
                c = pl.ds(h * 512, 512)
                w = jnp.concatenate(
                    [
                        wo[pl.ds(2 * g, 2), :, :, c].reshape(PAIR, 512),
                        wo[pl.ds(8 + 2 * g, 2), :, :, c].reshape(PAIR, 512),
                    ],
                    axis=0,
                )
                r = dot(a, w).reshape(4, 6, 8, 512)
                for f, (one, two) in enumerate(((0, 4), (1, 5), (2, 3))):
                    first = acc[f, js, 0, :, c] + r[:, one]
                    second = acc[f, js, 1, :, c] + r[:, two]
                    if last:
                        ob[f, js, :, c] = jnp.concatenate([first, second], axis=1).astype(BF16)
                    else:
                        acc[f, js, 0, :, c] = first
                        acc[f, js, 1, :, c] = second
            if last:
                out_copy(n).start()
            return carry

        lax.fori_loop(0, 4, project, 0)

    def final_step(g, carry):
        final(g, False)
        return carry

    lax.fori_loop(0, GROUPS - 1, final_step, 0)
    final(GROUPS - 1, True)

    to_sib.wait_send()
    for kind in range(2):
        for d in Z_ORDER:
            z_copy(kind, d).wait_send()
        for d in (1, 3, 2):
            y_copy(kind, d).wait_send()
        for d in range(4):
            for c in x_copies(kind, d):
                c.wait_send()
    for g in range(GROUPS):
        wo_copies(g)[1].wait_send()

    lax.fori_loop(24, 2 * (CHIPS - 1), tok_sent, 0)

    def share_sent(k, carry):
        for h in range(2):
            share_copy(h, k, tok.at[chip_by(k, -1), core]).wait_send()
        return carry

    lax.fori_loop(0, CHIPS, share_sent, 0)

    def back_sent(g, carry):
        def ret_sent(k, carry):
            for h in range(2):
                ret_copy(h, g, k).wait_send()
            return carry

        lax.fori_loop(0, CHIPS - 1, ret_sent, 0)
        for h in range(2):
            eb_copy(h, g).wait_send()
        return carry

    lax.fori_loop(0, GROUPS, back_sent, 0)
    for n in range(4):
        out_copy(n).wait()


def body(frames_in, gain_time, gain_space, w_tqkv, w_tout, w_sqkv, w_sout):
    dma = pltpu.SemaphoreType.DMA
    vmem = pl.BlockSpec(memory_space=pltpu.VMEM)
    hbm = pl.BlockSpec(memory_space=pl.ANY)
    out = pl.pallas_call(
        kernel,
        out_shape=jax.ShapeDtypeStruct((FRAMES, CHIPS, BLOCK, D), BF16),
        in_specs=[hbm, vmem, vmem, hbm, hbm, hbm, hbm],
        out_specs=hbm,
        scratch_shapes=[
            pltpu.VMEM((FRAMES, CHIPS, BLOCK, D), BF16),
            pltpu.VMEM((CHIPS, FRAMES, BLOCK, D), BF16),
            pltpu.VMEM((FRAMES, CHIPS, BLOCK, D), BF16),
            pltpu.VMEM((CHIPS, 2, FRAMES, BLOCK, D), BF16),
            pltpu.VMEM((D, 3 * D), BF16),
            pltpu.VMEM((D, D), BF16),
            pltpu.VMEM((32, 512), BF16),
            pltpu.VMEM((2, 32, 512), BF16),
            pltpu.VMEM((8, 2, 32, 512), BF16),
            pltpu.VMEM((GROUPS, CHIPS, 2, 32, 3 * PAIR), BF16),
            pltpu.VMEM((GROUPS, CHIPS, 2, 32, PAIR), BF16),
            pltpu.VMEM((CHIPS, 2, 32, D), BF16),
            pltpu.VMEM((FRAMES, CHIPS, 2, 8, D), F32),
            pltpu.VMEM((CHIPS * BLOCK, D), BF16),
            pltpu.VMEM((3, CHIPS * 48, PAIR), F32),
            pltpu.VMEM((GROUPS * 3, CHIPS * 48, PAIR), F32),
            pltpu.VMEM((GROUPS, CHIPS * 48, PAIR), F32),
            pltpu.VMEM((CHIPS * 48, PAIR), F32),
            pltpu.VMEM((GROUPS, CHIPS, FRAMES, BLOCK, 2 * PAIR), BF16),
            pltpu.VMEM((GROUPS, CHIPS, FRAMES, BLOCK, PAIR), BF16),
            pltpu.VMEM((GROUPS, CHIPS, FRAMES, BLOCK, 2 * PAIR), BF16),
            pltpu.VMEM((FRAMES, CHIPS, BLOCK, D), BF16),
            dma((11,)),
            dma((2,)),
            dma((2, 15)), dma((2, 15)),
            dma((2, 16)), dma((2, 16)),
            dma((2, 7)), dma((2, 7)),
            dma((2, 3)), dma((2, 3)),
            dma((2, 4)), dma((2, 4)),
            dma((2, 4)), dma((2, 4)),
            dma((4,)), dma((4,)),
            dma((8,)),
            dma((2, 4)), dma((2, 4)),
            dma((2, 4, 15)), dma((2, 4, 15)),
            dma((4,)),
        ],
        compiler_params=pltpu.CompilerParams(
            collective_id=0, has_side_effects=True, vmem_limit_bytes=56 * 2**20
        ),
        name="encoder_block",
    )(
        frames_in.reshape(FRAMES, CHIPS, BLOCK, D),
        gain_time.reshape(1, D),
        gain_space.reshape(1, D),
        w_tqkv, w_tout, w_sqkv, w_sout,
    )
    return out.reshape(FRAMES, CHIPS * BLOCK, D)


def solution(mesh):
    in_specs = (P(("clip", "tm"), None, None), P(), P(), P("tm", None), P("tm", None), P(), P())
    out_specs = P(("clip", "tm"), None, None)
    return jax.shard_map(body, mesh=mesh, in_specs=in_specs, out_specs=out_specs, check_vma=False)
```

time: 119 us -> 108 us (0.908)
  Pallas kernels: 116 us -> 105 us
    pallas_call x1, Pallas kernels: 116 us -> 105 us  [body(): pl.pallas_call(kernel, out_shape=jax.ShapeDtypeStruct((FRAMES, CHIPS, BLO...]
where the time goes in v2:
time: 108 us
  Pallas kernels  105 us (97%)
  local copies, waits for them, and re-layouts  2.67 us (2%)
    pallas_call x1, Pallas kernels, body(): pl.pallas_call(kernel, out_shape=jax.ShapeDtypeStruct((FRAMES, CHIPS, BLO...  105 us
    unnamed x1, local copies, waits for them, and re-layouts  2.67 us

profile of v2, /device:TPU:16, one launch (start us, length us, event | category | flops | bytes accessed | tf_op | source)
XLA Modules:
  0.0 107.8 jit_solution(16583478599566335188)
XLA Ops:
  0.0 105.1 %encoder_block.1 = bf16[3,16,16,1024]{3,2,1,0:T(8,128)(2,1)} custom-call(bf16[3,16,16,1024]{3,2,1,0:T(8,128)(2,1)} %bitcast.5, f32[1,1024]{1,0:T(1,128)} %bitcast.6, f32[1,1024]{1,0:T(1,128)} %bitcast.7, bf16[32,3072]{1,0:T(8,128)(2,1)} %wt_hbm.1, bf16[32,1024]{1,0:T(8,128)(2,1)} %wto_hbm.1, bf16[1024,3072]{1,0:T(8,128)(2,1)} %ws_hbm.1, ...), custom_call_target="tpu_custom_call" | custom-call | tf_op jit(solution)/shard_map/encoder_block/pallas_call | solution.py:560
  105.1 2.7 %copy.9 = bf16[3,256,1024]{2,1,0:T(8,128)(2,1)} copy(bf16[3,256,1024]{2,1,0:T(8,128)(2,1)} %bitcast.4) | data formatting | bytes 3145728

commit v3 on v2

--- a/solution.py
+++ b/solution.py
@@ -345,13 +345,13 @@
 
     def attend_patches(qkv, out):
         def patches(i, carry):
-            rows = [pl.ds(i * 4 + u, 96, stride=8) for u in range(4)]
+            rows = [pl.ds(i * 8 + u, 96, stride=8) for u in range(8)]
             triples = [(qkv(0, r), qkv(1, r).astype(BF16), qkv(2, r).astype(BF16)) for r in rows]
             for r, o in zip(rows, attend_pairs(triples)):
                 out[r, :] = o
             return carry
 
-        lax.fori_loop(0, 2, patches, 0)
+        patches(0, 0)
 
     here = pl.ds(pl.multiple_of(core * PAIR, PAIR), PAIR)
 
@@ -404,17 +404,16 @@
     lax.fori_loop(0, CHIPS, share_wait(1), 0)
 
     def second_group(g, carry):
-        def project(n, carry):
-            a = tok[pl.ds(n * 8, 8), :, 2].reshape(256, D)
+        def project():
+            a = tok[:, :, 2].reshape(512, D)
             r = dot(a, wt[g].reshape(D, 3 * PAIR))
             for t in range(3):
                 part = r[:, t * PAIR : (t + 1) * PAIR]
-                for i in range(16):
-                    at = pl.multiple_of((n * 16 + i) * 24 + 8, 8)
+                for i in range(32):
+                    at = i * 24 + 8
                     qb[g * 3 + t, pl.ds(at, 16), :] = part[i * 16 : i * 16 + 16]
-            return carry
-
-        lax.fori_loop(0, 2, project, 0)
+
+        project()
 
         @pl.when(g == 0)
         def _():

time: 108 us -> 106 us (0.981)
  Pallas kernels: 105 us -> 103 us
    pallas_call x1, Pallas kernels: 105 us -> 103 us  [body(): pl.pallas_call(kernel, out_shape=jax.ShapeDtypeStruct((FRAMES, CHIPS, BLO...]
where the time goes in v3:
time: 106 us
  Pallas kernels  103 us (97%)
  local copies, waits for them, and re-layouts  2.67 us (3%)
    pallas_call x1, Pallas kernels, body(): pl.pallas_call(kernel, out_shape=jax.ShapeDtypeStruct((FRAMES, CHIPS, BLO...  103 us
    unnamed x1, local copies, waits for them, and re-layouts  2.67 us

profile of v3, /device:TPU:16, one launch (start us, length us, event | category | flops | bytes accessed | tf_op | source)
XLA Modules:
  0.0 105.8 jit_solution(2561172730668758939)
XLA Ops:
  0.0 103.2 %encoder_block.1 = bf16[3,16,16,1024]{3,2,1,0:T(8,128)(2,1)} custom-call(bf16[3,16,16,1024]{3,2,1,0:T(8,128)(2,1)} %bitcast.5, f32[1,1024]{1,0:T(1,128)} %bitcast.6, f32[1,1024]{1,0:T(1,128)} %bitcast.7, bf16[32,3072]{1,0:T(8,128)(2,1)} %wt_hbm.1, bf16[32,1024]{1,0:T(8,128)(2,1)} %wto_hbm.1, bf16[1024,3072]{1,0:T(8,128)(2,1)} %ws_hbm.1, ...), custom_call_target="tpu_custom_call" | custom-call | tf_op jit(solution)/shard_map/encoder_block/pallas_call | solution.py:559
  103.2 2.7 %copy.9 = bf16[3,256,1024]{2,1,0:T(8,128)(2,1)} copy(bf16[3,256,1024]{2,1,0:T(8,128)(2,1)} %bitcast.4) | data formatting | bytes 3145728
